TPU v7x, 32 devices: a whole 2x2x4 slice. The times are simulated.
32 devices in a mesh: dp: 2 (over core), ctx: 8 (over z, y), tp: 2 (over x).
Axes of the slice: x: 2, y: 2, z: 4, core: 2. Of those that a mesh axis runs over, the one named last changes fastest.
Arguments:
- doc_lengths: int32 [2, 4], P('dp'), may hold values from 1 to 512, 1024 in all within a row
- piece_plan: int32 [2, 16], P('dp'), may hold values from 0 to 15, each once within a row
- queries: bfloat16 [2, 1024, 8192], P('dp', 'ctx', 'tp'), may hold values from -8 to 8
- rotated_keys: bfloat16 [2, 1024, 1024], P('dp', 'ctx', 'tp'), may hold values from -8 to 8
- value_matrix: bfloat16 [2, 1024, 1024], P('dp', 'ctx', 'tp'), may hold values from -6 to 6
- output_gradient: bfloat16 [2, 1024, 8192], P('dp', 'ctx', 'tp'), may hold values from -6 to 6
- attention_output: bfloat16 [2, 1024, 8192], P('dp', 'ctx', 'tp'), may hold values from -3 to 3
- value_projection_weight: bfloat16 [8192, 1024], P('dp', 'tp'), may hold values from -0.1875 to 0.1875
Outputs:
- query_grad: bfloat16 [2, 1024, 8192], P('dp', 'ctx', 'tp')
- key_gradient: bfloat16 [2, 1024, 1024], P('dp', 'ctx', 'tp')
- value_gradient: bfloat16 [2, 1024, 1024], P('dp', 'ctx', 'tp')
- input_grad: bfloat16 [2, 1024, 8192], P('dp', 'ctx', 'tp')
Inputs may be any that keep to these rules, and one draw needn't show every extreme that they name: `doc_lengths`: the 4 lengths of a micro-batch sum to 1024, and the longest is exactly half of 1024. `piece_plan`: each row names every stream piece of 64 tokens once.
All inputs are finite; a program needn't handle non-finite values.
Results may differ from a plain program's by a relative error of at most 0.012.
Values may be sent and summed in bfloat16 or wider, within the bound.
A program may use at most 128 MiB of HBM per device.

v0:
```python
import math

import jax
import jax.numpy as jnp
from jax import lax
from jax.sharding import PartitionSpec as P

QUERY_HEADS = 64
KEY_VALUE_HEADS = 8
HEAD_SIZE = 128
PIECE = 64


NEG = -1e30


def stream_layout(doc_lengths, piece_plan):
    slot_count = piece_plan.shape[0]
    piece_start = jnp.broadcast_to(piece_plan[:, None] * PIECE, (slot_count, PIECE))
    offsets = jnp.broadcast_to(jnp.arange(PIECE, dtype=jnp.int32)[None, :], (slot_count, PIECE))
    position = (piece_start + offsets).reshape(slot_count * PIECE)
    doc_ends = jnp.cumsum(doc_lengths)
    document = jnp.sum((position[:, None] >= doc_ends[None, :]).astype(jnp.int32), axis=1)
    return (position, document)


def split_blocks(row_count):
    block_rows = math.gcd(row_count, 512)
    return (block_rows, row_count // block_rows)


def on_device(
    doc_lengths,
    piece_plan,
    queries,
    rotated_keys,
    value_matrix,
    output_gradient,
    attention_output,
    value_projection_weight,
):
    position, document = stream_layout(doc_lengths[0], piece_plan[0])
    tok_rows = queries.shape[1]
    kv_width = rotated_keys.shape[2]
    kv_heads = kv_width // HEAD_SIZE
    queries_per_group = QUERY_HEADS // KEY_VALUE_HEADS
    temper = HEAD_SIZE ** (-0.5)
    first_row = lax.axis_index("ctx") * tok_rows
    own_pos = lax.dynamic_slice_in_dim(position, first_row, tok_rows)
    own_doc = lax.dynamic_slice_in_dim(document, first_row, tok_rows)
    head_queries = queries[0].reshape(tok_rows, kv_heads, queries_per_group, HEAD_SIZE)
    head_gradient = output_gradient[0].reshape(tok_rows, kv_heads, queries_per_group, HEAD_SIZE)
    head_output = attention_output[0].reshape(tok_rows, kv_heads, queries_per_group, HEAD_SIZE)
    row_delta = jnp.sum(
        head_gradient.astype(jnp.float32) * head_output.astype(jnp.float32), axis=-1
    ).transpose(1, 2, 0)

    def allowed_pairs(key_pos, key_doc):
        return (own_doc[:, None] == key_doc[None, :]) & (own_pos[:, None] >= key_pos[None, :])

    def block_scores(head_keys):
        return (
            jnp.einsum(
                "tkgd,skd->kgts", head_queries, head_keys, preferred_element_type=jnp.float32
            )
            * temper
        )

    def stats_step(running, key_block, key_pos, key_doc):
        row_max, row_sum = running
        allowed = allowed_pairs(key_pos, key_doc)
        head_keys = key_block.reshape(key_block.shape[0], kv_heads, HEAD_SIZE)
        masked = jnp.where(allowed, block_scores(head_keys), NEG)
        new_max = jnp.maximum(row_max, jnp.max(masked, axis=-1))
        fresh_sum = jnp.sum(jnp.where(allowed, jnp.exp(masked - new_max[..., None]), 0.0), axis=-1)
        return (new_max, row_sum * jnp.exp(row_max - new_max) + fresh_sum)

    def stats_visit(running, key_block, key_pos, key_doc):
        return stats_step(running, key_block, key_pos, key_doc)

    def grad_step(query_acc, key_block, value_block, key_pos, key_doc, log_norm):
        row_count = key_block.shape[0]
        head_keys = key_block.reshape(row_count, kv_heads, HEAD_SIZE)
        head_values = value_block.reshape(row_count, kv_heads, HEAD_SIZE)
        allowed = allowed_pairs(key_pos, key_doc)
        scores = block_scores(head_keys)
        weights = jnp.exp(jnp.where(allowed, scores - log_norm[..., None], NEG))
        weights_low = weights.astype(jnp.bfloat16)
        grad_weights = jnp.einsum(
            "tkgd,skd->kgts", head_gradient, head_values, preferred_element_type=jnp.float32
        )
        grad_scores = (weights * (grad_weights - row_delta[..., None]) * temper).astype(
            jnp.bfloat16
        )
        query_acc = query_acc + jnp.einsum(
            "kgts,skd->tkgd", grad_scores, head_keys, preferred_element_type=jnp.float32
        )
        key_part = jnp.einsum(
            "kgts,tkgd->skd", grad_scores, head_queries, preferred_element_type=jnp.float32
        ).reshape(row_count, kv_width)
        value_part = jnp.einsum(
            "kgts,tkgd->skd", weights_low, head_gradient, preferred_element_type=jnp.float32
        ).reshape(row_count, kv_width)
        return (query_acc, key_part, value_part)

    def grad_visit(query_acc, key_block, value_block, key_pos, key_doc, log_norm):
        return grad_step(query_acc, key_block, value_block, key_pos, key_doc, log_norm)

    start_max = jnp.full((kv_heads, queries_per_group, tok_rows), NEG, jnp.float32)
    start_sum = jnp.zeros((kv_heads, queries_per_group, tok_rows), jnp.float32)
    start_query = jnp.zeros((tok_rows, kv_heads, queries_per_group, HEAD_SIZE), jnp.float32)
    all_keys, all_values = (
        lax.all_gather(rotated_keys[0], "ctx", axis=0, tiled=True),
        lax.all_gather(value_matrix[0], "ctx", axis=0, tiled=True),
    )
    running = (start_max, start_sum)
    block_rows, block_count = split_blocks(all_keys.shape[0])

    def stats_advance(carried, member):
        return (stats_visit(carried, member[0], member[1], member[2]), None)

    running, unused = lax.scan(
        stats_advance,
        running,
        (
            all_keys.reshape(block_count, block_rows, kv_width),
            position.reshape(block_count, block_rows),
            document.reshape(block_count, block_rows),
        ),
    )
    row_max, row_sum = running
    log_norm = row_max + jnp.log(row_sum)
    query_acc = start_query
    row_count = all_keys.shape[0]
    block_rows, block_count = split_blocks(row_count)

    def grad_advance(carried, member):
        carried, key_part, value_part = grad_visit(
            carried, member[0], member[1], member[2], member[3], log_norm
        )
        return (carried, (key_part, value_part))

    query_acc, block_parts = lax.scan(
        grad_advance,
        query_acc,
        (
            all_keys.reshape(block_count, block_rows, kv_width),
            all_values.reshape(block_count, block_rows, kv_width),
            position.reshape(block_count, block_rows),
            document.reshape(block_count, block_rows),
        ),
    )
    query_acc, key_part, value_part = (
        query_acc,
        block_parts[0].reshape(row_count, kv_width),
        block_parts[1].reshape(row_count, kv_width),
    )
    key_sum, value_sum = (
        lax.psum_scatter(
            key_part.astype(jnp.bfloat16), "ctx", scatter_dimension=0, tiled=True
        ).astype(jnp.float32),
        lax.psum_scatter(
            value_part.astype(jnp.bfloat16), "ctx", scatter_dimension=0, tiled=True
        ).astype(jnp.float32),
    )
    key_gradient = key_sum.astype(jnp.bfloat16)
    value_gradient = value_sum.astype(jnp.bfloat16)
    query_grad = query_acc.astype(jnp.bfloat16).reshape(
        tok_rows, kv_heads * queries_per_group * HEAD_SIZE
    )
    partial_input = jnp.einsum(
        "tc,rc->tr",
        value_gradient,
        lax.all_gather(value_projection_weight, "dp", axis=0, tiled=True),
        preferred_element_type=jnp.float32,
    )
    input_grad = lax.psum_scatter(
        partial_input.astype(jnp.bfloat16), "tp", scatter_dimension=1, tiled=True
    )
    return (query_grad[None], key_gradient[None], value_gradient[None], input_grad[None])


def solution(mesh):
    in_specs = (
        P("dp", None),
        P("dp", None),
        P("dp", "ctx", "tp"),
        P("dp", "ctx", "tp"),
        P("dp", "ctx", "tp"),
        P("dp", "ctx", "tp"),
        P("dp", "ctx", "tp"),
        P("dp", "tp"),
    )
    out_specs = (
        P("dp", "ctx", "tp"),
        P("dp", "ctx", "tp"),
        P("dp", "ctx", "tp"),
        P("dp", "ctx", "tp"),
    )
    return jax.shard_map(
        on_device, mesh=mesh, in_specs=in_specs, out_specs=out_specs, check_vma=False
    )
```

profile of v0, /device:TPU:0, one launch (start us, length us, event | category | flops | bytes accessed | tf_op | source)
XLA Modules:
  0.0 324.1 jit_solution(12450606110571011405)
XLA Ops:
  15.7 3.0 copy.70
  20.6 33.3 %all-gather.8.cloned.1.call-done = bf16[1,1024,512]{2,1,0:T(8,128)(2,1)} async-done(((bf16[1,128,512]{2,1,0:T(8,128)(2,1)}), bf16[1,1024,512]{2,1,0:T(8,128)(2,1)}) %all-gather.8.cloned.1.call-update) | async-done | bytes 1048592 | tf_op jit(solution)/shard_map/all_gather | solution.py:113
  55.3 19.3 %while.28 = (s32[]{:T(128)}, f32[4,8,128]{2,1,0:T(8,128)S(1)}, f32[4,8,128]{2,1,0:T(8,128)S(1)}, s32[128]{0:T(128)S(1)}, s32[2,512]{1,0:T(2,128)S(1)}, /*index=5...) while((s32[]{:T(128)}, f32[4,8,128]{2,1,0:T(8,128)S(1)}, ...), condition=%wide.region_5.6_spmd.clone, body=%wide.region_2.0_spmd.clone.sunk | while | flops 553865216 | bytes 19821696 | solution.py:122
  55.6 4.7 %fusion.48 = (f32[4,8,128]{2,1,0:T(8,128)S(1)}, f32[4,512,128,8]{2,1,3,0:T(8,128)}) fusion(pred[128,512]{0,1:T(8,128)(4,1)S(1)} %compare_and_fusion.4, bf16[512,4,128,1]{0,2,3,1:T(8,128)(2,1)S(1)} %bitcast.146, bf16[128,4,8,128]{3,0,2,1:T(8,128)(2,1)S(1)} %get-tuple-element.506), kind=kOutput, calls=%fused_computation.2.clone.1 | convolution fusion | flops 543158272 | bytes 10043392 | tf_op jit(solution)/shard_map/while/body/eval_jaxpr/tkgd,skd->kgts/dot_general | solution.py:63
  60.3 4.7 %select_reduce_fusion.2 = f32[4,8,128]{2,1,0:T(8,128)S(1)} fusion(f32[4,512,128,8]{2,1,3,0:T(8,128)} %get-tuple-element.459, f32[4,8,128]{2,1,0:T(8,128)S(1)} %select_maximum_fusion.2, pred[128,512]{0,1:T(8,128)(4,1)S(1)} %compare_and_fusion.4), kind=kLoop, calls=%fused_computation.1.clone.1 | loop fusion | flops 10481664 | bytes 8486912 | tf_op jit(solution)/shard_map/while/body/eval_jaxpr/reduce_sum | solution.py:75
  65.3 4.7 %fusion.48 = (f32[4,8,128]{2,1,0:T(8,128)S(1)}, f32[4,512,128,8]{2,1,3,0:T(8,128)}) fusion(pred[128,512]{0,1:T(8,128)(4,1)S(1)} %compare_and_fusion.4, bf16[512,4,128,1]{0,2,3,1:T(8,128)(2,1)S(1)} %bitcast.146, bf16[128,4,8,128]{3,0,2,1:T(8,128)(2,1)S(1)} %get-tuple-element.506), kind=kOutput, calls=%fused_computation.2.clone.1 | convolution fusion | flops 543158272 | bytes 10043392 | tf_op jit(solution)/shard_map/while/body/eval_jaxpr/tkgd,skd->kgts/dot_general | solution.py:63
  70.0 4.6 %select_reduce_fusion.2 = f32[4,8,128]{2,1,0:T(8,128)S(1)} fusion(f32[4,512,128,8]{2,1,3,0:T(8,128)} %get-tuple-element.459, f32[4,8,128]{2,1,0:T(8,128)S(1)} %select_maximum_fusion.2, pred[128,512]{0,1:T(8,128)(4,1)S(1)} %compare_and_fusion.4), kind=kLoop, calls=%fused_computation.1.clone.1 | loop fusion | flops 10481664 | bytes 8486912 | tf_op jit(solution)/shard_map/while/body/eval_jaxpr/reduce_sum | solution.py:75
  74.6 20.3 %all-gather.10.cloned.1.call-done = bf16[1,1024,512]{2,1,0:T(8,128)(2,1)} async-done(((bf16[1,128,512]{2,1,0:T(8,128)(2,1)}), bf16[1,1024,512]{2,1,0:T(8,128)(2,1)}) %all-gather.10.cloned.1.call-update) | async-done | bytes 1048592 | tf_op jit(solution)/shard_map/all_gather | solution.py:114
  94.9 57.3 %while.29 = (s32[]{:T(128)}, f32[128,4,8,128]{0,3,2,1:T(8,128)}, bf16[2,512,512]{1,2,0:T(8,128)(2,1)}, bf16[2,512,512]{1,2,0:T(8,128)(2,1)}, bf16[2,512,512]{1,2...) while((s32[]{:T(128)}, f32[128,4,8,128]{0,3,2,1:T(8,128)}, ...), condition=%wide.region_8.9_spmd.clone, body=%wide.region_7.8_spmd.clone.sunk | while | flops 2708668416 | bytes 96204144 | solution.py:143
  95.2 4.5 %fusion.60 = f32[4,512,128,8]{2,1,3,0:T(8,128)} fusion(bf16[512,4,128,1]{0,2,3,1:T(8,128)(2,1)S(1)} %bitcast.142, bf16[128,4,8,128]{0,3,2,1:T(8,128)(2,1)S(1)} %get-tuple-element.550), kind=kOutput, calls=%fused_computation.38.clone.1 | convolution fusion | flops 536870912 | bytes 9961472 | tf_op jit(solution)/shard_map/while/body/eval_jaxpr/tkgd,skd->kgts/dot_general | solution.py:63
  100.8 6.8 %fusion.61 = bf16[4,8,128,512]{2,3,1,0:T(8,128)(2,1)S(1)} fusion(f32[4,512,128,8]{2,1,3,0:T(8,128)} %fusion.60, f32[4,8,128]{2,1,0:T(8,128)S(1)} %get-tuple-element.554, f32[4,8,128]{2,1,0:T(8,128)S(1)} %get-tuple-element.551, pred[128,512]{0,1:T(8,128)(4,1)S(1)} %compare_and_fusion.5, bf16[512,4,128,1]{0,2,3,1:T(8,128)(2,1)} %bitcast.149, ...), kind=kOutput, calls=%fused_computation.13.clone.1 | convolution fusion | flops 551550976 | bytes 14254080 | tf_op jit(solution)/shard_map/while/body/eval_jaxpr/tkgd,skd->kgts/dot_general | solution.py:89
  111.1 5.6 %fusion.62 = bf16[4,512,128,1]{1,2,3,0:T(8,128)(2,1)S(1)} fusion(bf16[128,4,8,128]{0,3,2,1:T(8,128)(2,1)S(1)} %copy-done.4, f32[4,512,128,8]{2,1,3,0:T(8,128)} %fusion.60, f32[4,8,128]{2,1,0:T(8,128)S(1)} %get-tuple-element.551, pred[128,512]{0,1:T(8,128)(4,1)S(1)} %compare_and_fusion.5), kind=kOutput, calls=%fused_computation.18.clone.1 | convolution fusion | flops 545259520 | bytes 10043392 | tf_op jit(solution)/shard_map/while/body/eval_jaxpr/kgts,tkgd->skd/dot_general | solution.py:101
  118.8 4.4 %bitcast_add_fusion.2 = f32[128,4,8,128]{0,3,2,1:T(8,128)} fusion(f32[128,4,8,128]{0,3,2,1:T(8,128)} %get-tuple-element.526, bf16[512,4,128,1]{0,2,3,1:T(8,128)(2,1)S(1)} %bitcast.143, bf16[4,8,128,512]{2,3,1,0:T(8,128)(2,1)} %copy-done, pred[]{:T(512)S(6)} %compare.7), kind=kOutput, calls=%fused_computation.20.clone.1 | convolution fusion | flops 537919488 | bytes 8912897 | tf_op jit(solution)/shard_map/while/body/eval_jaxpr/kgts,skd->tkgd/dot_general | solution.py:95
  123.5 4.5 %fusion.60 = f32[4,512,128,8]{2,1,3,0:T(8,128)} fusion(bf16[512,4,128,1]{0,2,3,1:T(8,128)(2,1)S(1)} %bitcast.142, bf16[128,4,8,128]{0,3,2,1:T(8,128)(2,1)S(1)} %get-tuple-element.550), kind=kOutput, calls=%fused_computation.38.clone.1 | convolution fusion | flops 536870912 | bytes 9961472 | tf_op jit(solution)/shard_map/while/body/eval_jaxpr/tkgd,skd->kgts/dot_general | solution.py:63
  129.1 6.8 %fusion.61 = bf16[4,8,128,512]{2,3,1,0:T(8,128)(2,1)S(1)} fusion(f32[4,512,128,8]{2,1,3,0:T(8,128)} %fusion.60, f32[4,8,128]{2,1,0:T(8,128)S(1)} %get-tuple-element.554, f32[4,8,128]{2,1,0:T(8,128)S(1)} %get-tuple-element.551, pred[128,512]{0,1:T(8,128)(4,1)S(1)} %compare_and_fusion.5, bf16[512,4,128,1]{0,2,3,1:T(8,128)(2,1)} %bitcast.149, ...), kind=kOutput, calls=%fused_computation.13.clone.1 | convolution fusion | flops 551550976 | bytes 14254080 | tf_op jit(solution)/shard_map/while/body/eval_jaxpr/tkgd,skd->kgts/dot_general | solution.py:89
  135.9 2.0 copy-done
  139.4 5.6 %fusion.62 = bf16[4,512,128,1]{1,2,3,0:T(8,128)(2,1)S(1)} fusion(bf16[128,4,8,128]{0,3,2,1:T(8,128)(2,1)S(1)} %copy-done.4, f32[4,512,128,8]{2,1,3,0:T(8,128)} %fusion.60, f32[4,8,128]{2,1,0:T(8,128)S(1)} %get-tuple-element.551, pred[128,512]{0,1:T(8,128)(4,1)S(1)} %compare_and_fusion.5), kind=kOutput, calls=%fused_computation.18.clone.1 | convolution fusion | flops 545259520 | bytes 10043392 | tf_op jit(solution)/shard_map/while/body/eval_jaxpr/kgts,tkgd->skd/dot_general | solution.py:101
  147.1 5.1 %bitcast_add_fusion.2 = f32[128,4,8,128]{0,3,2,1:T(8,128)} fusion(f32[128,4,8,128]{0,3,2,1:T(8,128)} %get-tuple-element.526, bf16[512,4,128,1]{0,2,3,1:T(8,128)(2,1)S(1)} %bitcast.143, bf16[4,8,128,512]{2,3,1,0:T(8,128)(2,1)} %copy-done, pred[]{:T(512)S(6)} %compare.7), kind=kOutput, calls=%fused_computation.20.clone.1 | convolution fusion | flops 537919488 | bytes 8912897 | tf_op jit(solution)/shard_map/while/body/eval_jaxpr/kgts,skd->tkgd/dot_general | solution.py:95
  152.2 2.3 copy.75
  155.1 2.4 copy.74
  157.6 59.3 %reduce-scatter.6.cloned.1.call-done = bf16[128,512]{1,0:T(8,128)(2,1)} async-done(((bf16[1024,512]{1,0:T(8,128)(2,1)}), bf16[128,512]{1,0:T(8,128)(2,1)}) %reduce-scatter.6.cloned.1.call-update) | async-done | bytes 131088 | tf_op jit(solution)/shard_map/reduce_scatter | solution.py:162
  216.9 7.6 %convolution_convert_fusion = bf16[128,8192]{1,0:T(8,128)(2,1)} fusion(bf16[128,512]{1,0:T(8,128)(2,1)} %reduce-scatter.6.cloned.1.call-done, bf16[8192,512]{1,0:T(8,128)(2,1)} %all-gather.6.cloned.1.call-done), kind=kOutput, calls=%fused_computation.30 | convolution fusion | flops 1074790400 | bytes 10616832 | tf_op jit(solution)/shard_map/tc,rc->tr/dot_general | solution.py:171
  226.0 57.5 %reduce-scatter.4.cloned.1.call-done = bf16[128,512]{1,0:T(8,128)(2,1)} async-done(((bf16[1024,512]{1,0:T(8,128)(2,1)}), bf16[128,512]{1,0:T(8,128)(2,1)}) %reduce-scatter.4.cloned.1.call-update) | async-done | bytes 131088 | tf_op jit(solution)/shard_map/reduce_scatter | solution.py:159
  283.5 33.5 %reduce-scatter.8.cloned.1.call-done = bf16[128,4096]{1,0:T(8,128)(2,1)} async-done(((bf16[128,8192]{1,0:T(8,128)(2,1)}), bf16[128,4096]{1,0:T(8,128)(2,1)}) %reduce-scatter.8.cloned.1.call-update) | async-done | bytes 1048592 | tf_op jit(solution)/shard_map/reduce_scatter | solution.py:177
  (99 shorter events, 25.4 us)
Async XLA Ops:
  8.0 45.8 %all-gather.8.cloned.1.call-start = ((), (), s32[]{:S(2)}) async-start(), calls=%async_computation.7 | async-start | bytes 1179648 | tf_op jit(solution)/shard_map/all_gather | solution.py:113
  8.7 86.2 %all-gather.10.cloned.1.call-start = ((), (), s32[]{:S(2)}) async-start(), calls=%async_computation.8 | async-start | bytes 1179648 | tf_op jit(solution)/shard_map/all_gather | solution.py:114
  9.5 207.4 %reduce-scatter.6.cloned.1.call-start = ((), (), s32[]{:S(2)}) async-start(), calls=%async_computation.4 | async-start | bytes 1179648 | tf_op jit(solution)/shard_map/reduce_scatter | solution.py:162
  15.7 38.2 %copy-start.3 = (bf16[1,128,4096]{1,2,0:T(8,128)(2,1)}, bf16[1,128,4096]{1,2,0:T(8,128)(2,1)S(1)}, u32[]{:S(2)}) copy-start(bf16[1,128,4096]{1,2,0:T(8,128)(2,1)S(1)} %copy.69) | copy-start | bytes 3145732
  94.9 4.8 %copy-start.2 = (bf16[2,512,512]{2,1,0:T(8,128)(2,1)S(1)}, bf16[2,512,512]{2,1,0:T(8,128)(2,1)}, u32[]{:S(2)}) copy-start(bf16[2,512,512]{2,1,0:T(8,128)(2,1)} %get-tuple-element.552) | copy-start | bytes 3145732 | tf_op jit(solution)/shard_map/while
  107.6 2.0 copy-start
  109.6 1.5 copy-start.4
  111.1 5.7 %copy-start.5 = (bf16[2,512,512]{1,2,0:T(8,128)(2,1)S(1)}, bf16[2,512,512]{1,2,0:T(8,128)(2,1)}, u32[]{:S(2)}) copy-start(bf16[2,512,512]{1,2,0:T(8,128)(2,1)} %get-tuple-element.527) | copy-start | bytes 3145732 | tf_op jit(solution)/shard_map/while
  111.1 5.7 %copy-start.7 = (bf16[2,512,512]{1,2,0:T(8,128)(2,1)S(1)}, bf16[2,512,512]{1,2,0:T(8,128)(2,1)}, u32[]{:S(2)}) copy-start(bf16[2,512,512]{1,2,0:T(8,128)(2,1)} %get-tuple-element.528) | copy-start | bytes 3145732 | tf_op jit(solution)/shard_map/while
  116.8 1.0 copy-start.6
  117.8 1.0 copy-start.8
  123.2 4.8 %copy-start.2 = (bf16[2,512,512]{2,1,0:T(8,128)(2,1)S(1)}, bf16[2,512,512]{2,1,0:T(8,128)(2,1)}, u32[]{:S(2)}) copy-start(bf16[2,512,512]{2,1,0:T(8,128)(2,1)} %get-tuple-element.552) | copy-start | bytes 3145732 | tf_op jit(solution)/shard_map/while
  135.9 2.0 copy-start
  137.9 1.5 copy-start.4
  139.4 5.7 %copy-start.5 = (bf16[2,512,512]{1,2,0:T(8,128)(2,1)S(1)}, bf16[2,512,512]{1,2,0:T(8,128)(2,1)}, u32[]{:S(2)}) copy-start(bf16[2,512,512]{1,2,0:T(8,128)(2,1)} %get-tuple-element.527) | copy-start | bytes 3145732 | tf_op jit(solution)/shard_map/while
  139.4 5.7 %copy-start.7 = (bf16[2,512,512]{1,2,0:T(8,128)(2,1)S(1)}, bf16[2,512,512]{1,2,0:T(8,128)(2,1)}, u32[]{:S(2)}) copy-start(bf16[2,512,512]{1,2,0:T(8,128)(2,1)} %get-tuple-element.528) | copy-start | bytes 3145732 | tf_op jit(solution)/shard_map/while
  145.1 1.0 copy-start.6
  146.1 1.0 copy-start.8
  154.5 62.4 %all-gather.6.cloned.1.call-start = ((), (), s32[]{:S(2)}) async-start(), calls=%async_computation.5 | async-start | bytes 12582912 | tf_op jit(solution)/shard_map/all_gather | solution.py:174
  155.1 69.5 %copy-start.1 = (f32[128,4,8,128]{0,3,2,1:T(8,128)S(1)}, f32[128,4,8,128]{0,3,2,1:T(8,128)}, u32[]{:S(2)}) copy-start(f32[128,4,8,128]{0,3,2,1:T(8,128)} %get-tuple-element.128) | copy-start | bytes 6291460
  155.1 128.4 %reduce-scatter.4.cloned.1.call-start = ((), (), s32[]{:S(2)}) async-start(), calls=%async_computation.3 | async-start | bytes 1179648 | tf_op jit(solution)/shard_map/reduce_scatter | solution.py:159
  157.6 159.4 %reduce-scatter.8.cloned.1.call-start = ((), (), s32[]{:S(2)}) async-start(), calls=%async_computation.6 | async-start | bytes 3145728 | tf_op jit(solution)/shard_map/reduce_scatter | solution.py:177
Sparse Core Ops, SparseCore 0:
  11.0 42.8 all-gather.7
  56.0 38.8 all-gather.9
  154.6 62.2 reduce-scatter.5
  221.1 62.3 reduce-scatter.3
  286.1 30.8 reduce-scatter.7
Sparse Core Ops, SparseCore 1:
  156.5 18.5 all-gather.5
where the time goes:
time: 324 us
  waiting for transfers between devices  206 us (64%)
  matrix products  63.3 us (20%)
  local copies, waits for them, and re-layouts  25.4 us (8%)
  between operations  15.3 us (5%)
  other arithmetic  13.8 us (4%)
    reduce_scatter x1, waiting for transfers between devices, on_device(): lax.psum_scatter(value_part.astype(jnp.bfloat16), 'ctx', scatter_dimensio...  59.3 us
    reduce_scatter x1, waiting for transfers between devices, on_device(): lax.psum_scatter(key_part.astype(jnp.bfloat16), 'ctx', scatter_dimension=...  57.5 us
    reduce_scatter x1, waiting for transfers between devices, on_device(): lax.psum_scatter(partial_input.astype(jnp.bfloat16), 'tp', scatter_dimens...  33.5 us
    all_gather x1, waiting for transfers between devices, on_device(): lax.all_gather(rotated_keys[0], 'ctx', axis=0, tiled=True)  33.3 us
    all_gather x1, waiting for transfers between devices, on_device(): lax.all_gather(value_matrix[0], 'ctx', axis=0, tiled=True)  20.3 us
    dot_general x4, matrix products, block_scores(): jnp.einsum('tkgd,skd->kgts', head_queries, head_keys, preferred_element_t...  18.4 us
    dot_general x2, matrix products, grad_step(): jnp.einsum('tkgd,skd->kgts', head_gradient, head_values, preferred_elemen...  13.6 us
    dot_general x2, matrix products, grad_step(): jnp.einsum('kgts,tkgd->skd', weights_low, head_gradient, preferred_elemen...  11.3 us
  transfers between devices with their start and end apart: 6, of which 5 were waited for; matrix products, arithmetic and copies ran while one was open for 13% of the time, Pallas kernels for 0%

commit v1 on v0

v1 whole, which is shorter than its diff:
```python
import functools
import math

import jax
import jax.numpy as jnp
from jax import lax
from jax.experimental import pallas as pl
from jax.experimental.pallas import tpu as pltpu
from jax.sharding import PartitionSpec as P

QUERY_HEADS = 64
KEY_VALUE_HEADS = 8
HEAD_SIZE = 128
PIECE = 64
NEG = -1e30
MESH = pl.DeviceIdType.MESH
NT = (((1,), (1,)), ((), ()))
TN = (((0,), (0,)), ((), ()))
VMEM_LIMIT = 56 * 1024 * 1024


def ring_place(index, n):
    odd = index % 2
    return (1 - odd) * (index // 2) + odd * (n - 1 - index // 2)


def ring_member(place, n):
    back = place // (n // 2)
    return (1 - back) * (2 * place) + back * (2 * (n - place) - 1)


def around(n):
    me = lax.axis_index("ctx")
    place = ring_place(me, n)

    def member(offset):
        return ring_member((place + offset + 2 * n) % n, n)

    return me, member


def gather_kernel(n, k_ref, v_ref, k_all, v_all, send_sem, recv_sem, own_sem):
    me, member = around(n)
    right, left = member(1), member(-1)
    barrier = pltpu.get_barrier_semaphore()
    for peer in (left, right):
        pl.semaphore_signal(barrier, inc=1, device_id={"ctx": peer}, device_id_type=MESH)
    own = [
        pltpu.make_async_copy(k_ref, k_all.at[me], own_sem.at[0]),
        pltpu.make_async_copy(v_ref, v_all.at[me], own_sem.at[1]),
    ]
    for copy in own:
        copy.start()
    pl.semaphore_wait(barrier, 2)
    long, short = n // 2, (n - 1) // 2
    streams = []
    for tensor, (source, target) in enumerate(((k_ref, k_all), (v_ref, v_all))):
        streams.append((source, target, 1, long if tensor == 0 else short, 2 * tensor))
        streams.append((source, target, -1, short if tensor == 0 else long, 2 * tensor + 1))
    copies = {}
    for step in range(long):
        for source, target, way, count, row in streams:
            if step >= count:
                continue
            block = member(-way * step)
            if step > 0:
                copies[row, step - 1].wait_recv()
            copy = pltpu.make_async_remote_copy(
                src_ref=source if step == 0 else target.at[block],
                dst_ref=target.at[block],
                send_sem=send_sem.at[row, step],
                recv_sem=recv_sem.at[row, step],
                device_id={"ctx": right if way == 1 else left},
                device_id_type=MESH,
            )
            copy.start()
            copies[row, step] = copy
    for source, target, way, count, row in streams:
        copies[row, count - 1].wait_recv()
    for copy in copies.values():
        copy.wait_send()
    for copy in own:
        copy.wait()


def gather(keys, values, n):
    rows, width = keys.shape
    whole = jax.ShapeDtypeStruct((n, rows, width), keys.dtype)
    steps = n // 2
    return pl.pallas_call(
        functools.partial(gather_kernel, n),
        out_shape=(whole, whole),
        in_specs=[pl.BlockSpec(memory_space=pl.ANY)] * 2,
        out_specs=[pl.BlockSpec(memory_space=pl.ANY)] * 2,
        scratch_shapes=[
            pltpu.SemaphoreType.DMA((4, steps)),
            pltpu.SemaphoreType.DMA((4, steps)),
            pltpu.SemaphoreType.DMA((2,)),
        ],
        compiler_params=pltpu.CompilerParams(collective_id=0, has_side_effects=True),
        name="gather_kv",
    )(keys, values)


def attention_kernel(
    pairs,
    chunk,
    lengths,
    plan,
    first_slot,
    q_ref,
    g_ref,
    o_ref,
    k_ref,
    v_ref,
    dq_ref,
    dk_ref,
    dv_ref,
    bias,
    scores,
    dk_acc,
    dv_acc,
):
    group, pair = pl.program_id(0), pl.program_id(1)
    keys, toks = bias.shape
    chunks = keys // chunk
    heads = q_ref.shape[1] // HEAD_SIZE

    @pl.when((group == 0) & (pair == 0))
    def _():
        lane = lax.broadcasted_iota(jnp.int32, (1, toks), 1)
        row_pos = jnp.zeros((1, toks), jnp.int32)
        for piece in range(toks // PIECE):
            here = plan[first_slot[0] + piece] * PIECE + lane - piece * PIECE
            row_pos = jnp.where(lane // PIECE == piece, here, row_pos)
        start = jnp.zeros((1, toks), jnp.int32)
        end = jnp.int32(0)
        for doc in range(lengths.shape[0]):
            end = end + lengths[doc]
            start = jnp.where(row_pos >= end, end, start)

        def fill(slot, carry):
            key_pos = plan[slot] * PIECE + lax.broadcasted_iota(jnp.int32, (PIECE, toks), 0)
            allowed = (key_pos >= start) & (key_pos <= row_pos)
            bias[pl.ds(pl.multiple_of(slot * PIECE, PIECE), PIECE), :] = jnp.where(allowed, 0.0, NEG)
            return carry

        lax.fori_loop(0, keys // PIECE, fill, 0)

    def stacked(ref):
        return jnp.concatenate(
            [ref[:, h * HEAD_SIZE : (h + 1) * HEAD_SIZE] for h in range(heads)], axis=0
        )

    queries, grads = stacked(q_ref), stacked(g_ref)
    product = grads.astype(jnp.float32) * stacked(o_ref).astype(jnp.float32)
    delta = jnp.sum(product.T, axis=0, keepdims=True)
    temper = HEAD_SIZE**-0.5
    scale = temper * math.log2(math.e)
    top = None
    for c in range(chunks):
        span = pl.ds(c * chunk, chunk)
        raw = lax.dot_general(k_ref[span, :], queries, NT, preferred_element_type=jnp.float32)
        block = raw * scale + jnp.concatenate([bias[span, :]] * heads, axis=1)
        scores[span, :] = block
        high = jnp.max(block.reshape(chunk // 8, 8, block.shape[1]), axis=0)
        top = high if top is None else jnp.maximum(top, high)
    top = jnp.max(top, axis=0, keepdims=True)
    total = None
    for c in range(chunks):
        span = pl.ds(c * chunk, chunk)
        block = jnp.exp2(scores[span, :] - top)
        scores[span, :] = block
        low = jnp.sum(block.reshape(chunk // 8, 8, block.shape[1]), axis=0)
        total = low if total is None else total + low
    inverse = 1.0 / jnp.sum(total, axis=0, keepdims=True)
    dq = None
    for c in range(chunks):
        span = pl.ds(c * chunk, chunk)
        weights = scores[span, :] * inverse
        grad_weights = lax.dot_general(
            v_ref[span, :], grads, NT, preferred_element_type=jnp.float32
        )
        dv = jnp.dot(weights.astype(jnp.bfloat16), grads, preferred_element_type=jnp.float32)
        grad_scores = (weights * ((grad_weights - delta) * temper)).astype(jnp.bfloat16)
        dk = jnp.dot(grad_scores, queries, preferred_element_type=jnp.float32)
        part = lax.dot_general(
            grad_scores, k_ref[span, :], TN, preferred_element_type=jnp.float32
        )
        dq = part if dq is None else dq + part

        @pl.when(pair == 0)
        def _():
            dv_acc[span, :] = dv
            dk_acc[span, :] = dk

        @pl.when(pair > 0)
        def _():
            dv_acc[span, :] += dv
            dk_acc[span, :] += dk

    for h in range(heads):
        dq_ref[:, h * HEAD_SIZE : (h + 1) * HEAD_SIZE] = dq[h * toks : (h + 1) * toks].astype(
            dq_ref.dtype
        )

    @pl.when(pair == pairs - 1)
    def _():
        dk_ref[...] = dk_acc[...].astype(dk_ref.dtype)
        dv_ref[...] = dv_acc[...].astype(dv_ref.dtype)


def attention(lengths, plan, first_slot, queries, grads, outputs, keys, values):
    toks, q_width = queries.shape
    rows, kv_width = keys.shape
    kv_heads = kv_width // HEAD_SIZE
    per_group = q_width // kv_width
    heads = 2
    pairs = per_group // heads
    chunk = 256
    wide = pl.BlockSpec((toks, heads * HEAD_SIZE), lambda g, p, *_: (0, g * pairs + p))
    tall = pl.BlockSpec((rows, HEAD_SIZE), lambda g, p, *_: (0, g))
    cols = heads * toks
    return pl.pallas_call(
        functools.partial(attention_kernel, pairs, chunk),
        grid_spec=pltpu.PrefetchScalarGridSpec(
            num_scalar_prefetch=3,
            grid=(kv_heads, pairs),
            in_specs=[wide, wide, wide, tall, tall],
            out_specs=[wide, tall, tall],
            scratch_shapes=[
                pltpu.VMEM((rows, toks), jnp.float32),
                pltpu.VMEM((rows, cols), jnp.float32),
                pltpu.VMEM((rows, HEAD_SIZE), jnp.float32),
                pltpu.VMEM((rows, HEAD_SIZE), jnp.float32),
            ],
        ),
        out_shape=(
            jax.ShapeDtypeStruct((toks, q_width), queries.dtype),
            jax.ShapeDtypeStruct((rows, kv_width), keys.dtype),
            jax.ShapeDtypeStruct((rows, kv_width), keys.dtype),
        ),
        compiler_params=pltpu.CompilerParams(vmem_limit_bytes=VMEM_LIMIT),
        name="attention_backward",
    )(lengths, plan, first_slot, queries, grads, outputs, keys, values)


def reduce_kernel(
    n,
    n_tp,
    chunk,
    k_part,
    v_part,
    w_ref,
    dk_ref,
    dv_ref,
    di_ref,
    weight,
    ring_send,
    ring_recv,
    part_send,
    part_recv,
    ring_send_sem,
    ring_recv_sem,
    part_send_sem,
    part_recv_sem,
    w_sem,
):
    me, member = around(n)
    dp, tp = lax.axis_index("dp"), lax.axis_index("tp")
    other = 1 - dp
    right, left = member(1), member(-1)
    half = w_ref.shape[0]
    share = 2 * half // n_tp
    chunks = share // chunk
    barrier = pltpu.get_barrier_semaphore()
    for peer in (left, right):
        pl.semaphore_signal(barrier, inc=1, device_id={"ctx": peer}, device_id_type=MESH)
    pl.semaphore_signal(barrier, inc=1, device_id={"dp": other}, device_id_type=MESH)
    for k in range(1, n_tp):
        pl.semaphore_signal(barrier, inc=1, device_id={"tp": (tp + k) % n_tp}, device_id_type=MESH)
    own_rows = pl.ds(pl.multiple_of(dp * half, half), half)
    w_own = pltpu.make_async_copy(w_ref, weight.at[own_rows], w_sem.at[0])
    w_own.start()
    pl.semaphore_wait(barrier, 2 + n_tp)
    w_copy = pltpu.make_async_remote_copy(
        src_ref=w_ref,
        dst_ref=weight.at[own_rows],
        send_sem=w_sem.at[1],
        recv_sem=w_sem.at[2],
        device_id={"dp": other},
        device_id_type=MESH,
    )
    long, short = n // 2, (n - 1) // 2
    copies = []
    rings = {}

    def ring_step(tensor, part, way, count, step):
        row = 2 * tensor + (0 if way == 1 else 1)
        place = member(way * (count - step))
        block = part[place].astype(jnp.float32)
        if step > 0:
            rings[row, step - 1].wait_recv()
            block = block + ring_recv[row, step - 1].astype(jnp.float32)
        ring_send[row, step] = block.astype(jnp.bfloat16)
        copy = pltpu.make_async_remote_copy(
            src_ref=ring_send.at[row, step],
            dst_ref=ring_recv.at[row, step],
            send_sem=ring_send_sem.at[row, step],
            recv_sem=ring_recv_sem.at[row, step],
            device_id={"ctx": right if way == 1 else left},
            device_id_type=MESH,
        )
        copy.start()
        rings[row, step] = copy
        copies.append(copy)

    def ring_end(tensor, part, counts):
        block = part[me].astype(jnp.float32)
        for at, count in enumerate(counts):
            rings[2 * tensor + at, count - 1].wait_recv()
            block = block + ring_recv[2 * tensor + at, count - 1].astype(jnp.float32)
        return block.astype(jnp.bfloat16)

    for step in range(long):
        ring_step(1, v_part, 1, long, step)
        if step < short:
            ring_step(1, v_part, -1, short, step)
        if step == 0:
            w_copy.start()
    ring_step(0, k_part, 1, short, 0)
    ring_step(0, k_part, -1, long, 0)
    value_grad = ring_end(1, v_part, (long, short))
    dv_ref[...] = value_grad
    w_own.wait()
    w_copy.wait()

    def product(part, c):
        rows = pl.ds(pl.multiple_of(part * share + c * chunk, chunk), chunk)
        return lax.dot_general(
            value_grad, weight[rows, :], NT, preferred_element_type=jnp.float32
        ).astype(jnp.bfloat16)

    pending = list(range(1, long))

    def key_step():
        if pending:
            step = pending.pop(0)
            if step < short:
                ring_step(0, k_part, 1, short, step)
            ring_step(0, k_part, -1, long, step)

    parts = {}
    done = 0
    for c in range(chunks):
        for k in range(1, n_tp):
            peer = (tp + k) % n_tp
            part_send[k - 1, c] = product(peer, c)
            copy = pltpu.make_async_remote_copy(
                src_ref=part_send.at[k - 1, c],
                dst_ref=part_recv.at[k - 1, c],
                send_sem=part_send_sem.at[k - 1, c],
                recv_sem=part_recv_sem.at[k - 1, c],
                device_id={"tp": peer},
                device_id_type=MESH,
            )
            copy.start()
            parts[k, c] = copy
            copies.append(copy)
            done += 1
            if done % 3 == 0:
                key_step()
    while pending:
        key_step()
    for c in range(chunks):
        total = product(tp, c).astype(jnp.float32)
        for k in range(1, n_tp):
            parts[k, c].wait_recv()
            total = total + part_recv[k - 1, c].astype(jnp.float32)
        di_ref[:, c * chunk : (c + 1) * chunk] = total.astype(jnp.bfloat16)
    dk_ref[...] = ring_end(0, k_part, (short, long))
    for copy in copies:
        copy.wait_send()


def reduce(key_part, value_part, weight, n, n_tp):
    rows, width = key_part.shape[0] // n, key_part.shape[1]
    half = weight.shape[0]
    share = 2 * half // n_tp
    chunk = 512
    chunks = share // chunk
    steps = n // 2
    vmem = pl.BlockSpec(memory_space=pltpu.VMEM)
    narrow = jax.ShapeDtypeStruct((rows, width), jnp.bfloat16)
    return pl.pallas_call(
        functools.partial(reduce_kernel, n, n_tp, chunk),
        out_shape=(narrow, narrow, jax.ShapeDtypeStruct((rows, share), jnp.bfloat16)),
        in_specs=[vmem, vmem, pl.BlockSpec(memory_space=pl.ANY)],
        out_specs=[vmem] * 3,
        scratch_shapes=[
            pltpu.VMEM((2 * half, width), jnp.bfloat16),
            pltpu.VMEM((4, steps, rows, width), jnp.bfloat16),
            pltpu.VMEM((4, steps, rows, width), jnp.bfloat16),
            pltpu.VMEM((n_tp - 1, chunks, rows, chunk), jnp.bfloat16),
            pltpu.VMEM((n_tp - 1, chunks, rows, chunk), jnp.bfloat16),
            pltpu.SemaphoreType.DMA((4, steps)),
            pltpu.SemaphoreType.DMA((4, steps)),
            pltpu.SemaphoreType.DMA((n_tp - 1, chunks)),
            pltpu.SemaphoreType.DMA((n_tp - 1, chunks)),
            pltpu.SemaphoreType.DMA((3,)),
        ],
        compiler_params=pltpu.CompilerParams(
            collective_id=1, has_side_effects=True, vmem_limit_bytes=VMEM_LIMIT
        ),
        name="reduce_gradients",
    )(key_part.reshape(n, rows, width), value_part.reshape(n, rows, width), weight)


def solution(mesh):
    n, n_tp = mesh.shape["ctx"], mesh.shape["tp"]

    def on_device(lengths, plan, queries, keys, values, grads, outputs, weight):
        toks, width = keys.shape[1:]
        all_keys, all_values = gather(keys[0], values[0], n)
        first_slot = (lax.axis_index("ctx") * (toks // PIECE)).astype(jnp.int32).reshape(1)
        query_grad, key_part, value_part = attention(
            lengths[0],
            plan[0],
            first_slot,
            queries[0],
            grads[0],
            outputs[0],
            all_keys.reshape(n * toks, width),
            all_values.reshape(n * toks, width),
        )
        key_grad, value_grad, input_grad = reduce(key_part, value_part, weight, n, n_tp)
        return query_grad[None], key_grad[None], value_grad[None], input_grad[None]

    spread = P("dp", "ctx", "tp")
    return jax.shard_map(
        on_device,
        mesh=mesh,
        in_specs=(P("dp", None), P("dp", None)) + (spread,) * 5 + (P("dp", "tp"),),
        out_specs=(spread,) * 4,
        check_vma=False,
    )
```

time: 324 us -> 117 us (0.36)
  waiting for transfers between devices: 206 us -> 0 us
  Pallas kernels: 0 us -> 111 us
  matrix products: 63.3 us -> 0 us
  local copies, waits for them, and re-layouts: 25.4 us -> 5.42 us
  between operations: 15.3 us -> 0.65 us
  other arithmetic: 13.8 us -> 0 us
    reduce_scatter x3 -> x0, waiting for transfers between devices: 150 us -> none  [the longest x1 59.3 us: on_device(): lax.psum_scatter(value_part.astype(jnp.bfloat16), 'ctx', scatter_dimensio...]
    pallas_call x0 -> x3, Pallas kernels: none -> 111 us  [the longest x1 44.2 us: reduce(): pl.pallas_call(functools.partial(reduce_kernel, n, n_tp, chunk), out_shap...]
    dot_general x13 -> x0, matrix products: 63.3 us -> none  [the longest x4 18.4 us: block_scores(): jnp.einsum('tkgd,skd->kgts', head_queries, head_keys, preferred_element_t...]
    all_gather x3 -> x0, waiting for transfers between devices: 53.5 us -> none  [the longest x1 33.3 us: on_device(): lax.all_gather(rotated_keys[0], 'ctx', axis=0, tiled=True)]
    reduce_sum x4 -> x0, other arithmetic: 11.2 us -> none  [the longest x2 9.24 us: stats_step(): jnp.sum(jnp.where(allowed, jnp.exp(masked - new_max[..., None]), 0.0), ax...]
    while x30 -> x0, local copies, waits for them, and re-layouts: 7.83 us -> none
    convert_element_type x3 -> x0, local copies, waits for them, and re-layouts: 7.69 us -> none  [the longest x1 2.99 us: on_device(): head_output.astype(jnp.float32)]
  transfers between devices with their start and end apart: 6 -> 0, of which waited for: 5 -> 0; matrix products, arithmetic and copies ran while one was open for 13% -> 0% of each run, Pallas kernels for 0% -> 0%
where the time goes in v1:
time: 117 us
  Pallas kernels  111 us (95%)
  local copies, waits for them, and re-layouts  5.42 us (5%)
    pallas_call x1, Pallas kernels, reduce(): pl.pallas_call(functools.partial(reduce_kernel, n, n_tp, chunk), out_shap...  44.2 us
    pallas_call x1, Pallas kernels, attention(): pl.pallas_call(functools.partial(attention_kernel, pairs, chunk), grid_sp...  39 us
    pallas_call x1, Pallas kernels, gather(): pl.pallas_call(functools.partial(gather_kernel, n), out_shape=(whole, who...  27.7 us
    unnamed x3, local copies, waits for them, and re-layouts  5.42 us

profile of v1, /device:TPU:0, one launch (start us, length us, event | category | flops | bytes accessed | tf_op | source)
XLA Modules:
  0.0 117.1 jit_solution(6329657839893587227)
XLA Ops:
  0.6 27.7 %gather_kv.1 = (bf16[8,128,512]{2,1,0:T(8,128)(2,1)}, bf16[8,128,512]{2,1,0:T(8,128)(2,1)}) custom-call(bf16[128,512]{1,0:T(8,128)(2,1)} %bitcast.24, bf16[128,512]{1,0:T(8,128)(2,1)} %bitcast.25), custom_call_target="tpu_custom_call" | custom-call | tf_op jit(solution)/shard_map/gather_kv/pallas_call | solution.py:90
  28.4 39.0 %attention_backward.1 = (bf16[128,4096]{1,0:T(8,128)(2,1)}, bf16[1024,512]{1,0:T(8,128)(2,1)}, bf16[1024,512]{1,0:T(8,128)(2,1)}) custom-call(s32[4]{0:T(128)} %bitcast.28, s32[16]{0:T(128)} %bitcast.29, s32[1]{0:T(128)} %bitcast.2.first_slot, bf16[128,4096]{1,0:T(8,128)(2,1)} %bitcast.17, bf16[128,4096]{1,0:T(8,128)(2,1)} %bitcast.18, ...), custom_call_target="tpu_custom_call" | custom-call | tf_op jit(solution)/shard_map/attention_backward/pallas_call | solution.py:224
  67.4 44.2 %reduce_gradients.1 = (bf16[128,512]{1,0:T(8,128)(2,1)}, bf16[128,512]{1,0:T(8,128)(2,1)}, bf16[128,4096]{1,0:T(8,128)(2,1)}) custom-call(bf16[8,128,512]{2,1,0:T(8,128)(2,1)} %bitcast.20, bf16[8,128,512]{2,1,0:T(8,128)(2,1)} %bitcast.21, bf16[4096,512]{1,0:T(8,128)(2,1)} %w_ref.1), custom_call_target="tpu_custom_call" | custom-call | tf_op jit(solution)/shard_map/reduce_gradients/pallas_call | solution.py:395
  111.7 1.6 %copy.15 = bf16[1,128,512]{2,1,0:T(8,128)(2,1)} copy(bf16[1,128,512]{2,1,0:T(8,128)(2,1)} %bitcast.27) | data formatting | bytes 262144
  113.2 1.6 %copy.16 = bf16[1,128,512]{2,1,0:T(8,128)(2,1)} copy(bf16[1,128,512]{2,1,0:T(8,128)(2,1)} %bitcast.26) | data formatting | bytes 262144
  114.8 2.3 %copy.17 = bf16[1,128,4096]{2,1,0:T(8,128)(2,1)} copy(bf16[1,128,4096]{2,1,0:T(8,128)(2,1)} %bitcast.16) | data formatting | bytes 2097152

commit v2 on v0

v2 whole, which is shorter than its diff:
```python
import functools
import math

import jax
import jax.numpy as jnp
from jax import lax
from jax.experimental import pallas as pl
from jax.experimental.pallas import tpu as pltpu
from jax.sharding import PartitionSpec as P

QUERY_HEADS = 64
KEY_VALUE_HEADS = 8
HEAD_SIZE = 128
PIECE = 64
NEG = -1e30
MESH = pl.DeviceIdType.MESH
NT = (((1,), (1,)), ((), ()))
TN = (((0,), (0,)), ((), ()))
VMEM_LIMIT = 56 * 1024 * 1024


def ring_place(index, n):
    odd = index % 2
    return (1 - odd) * (index // 2) + odd * (n - 1 - index // 2)


def ring_member(place, n):
    back = place // (n // 2)
    return (1 - back) * (2 * place) + back * (2 * (n - place) - 1)


def around(n):
    me = lax.axis_index("ctx")
    place = ring_place(me, n)

    def member(offset):
        return ring_member((place + offset + 2 * n) % n, n)

    return me, member


def fused_kernel(
    n,
    n_tp,
    chunk,
    lengths,
    plan,
    q_hbm,
    g_hbm,
    o_hbm,
    k_hbm,
    v_hbm,
    w_hbm,
    dq_ref,
    dk_ref,
    dv_ref,
    di_ref,
    q_wide,
    g_wide,
    o_wide,
    k_all,
    v_all,
    queries,
    grads,
    delta,
    bias,
    scores,
    top,
    inverse,
    dq_acc,
    k_part,
    v_part,
    value_grad,
    weight,
    ring_send,
    ring_recv,
    part_send,
    part_recv,
    load_sem,
    ag_send_sem,
    ag_recv_sem,
    ring_send_sem,
    ring_recv_sem,
    part_send_sem,
    part_recv_sem,
    w_sem,
):
    me, member = around(n)
    dp, tp = lax.axis_index("dp"), lax.axis_index("tp")
    other = 1 - dp
    right, left = member(1), member(-1)
    toks, kv_width = k_hbm.shape
    kv_heads = kv_width // HEAD_SIZE
    per_group = q_hbm.shape[1] // kv_width
    cols = per_group * toks
    half = w_hbm.shape[0]
    share = 2 * half // n_tp
    chunks = share // chunk
    long, short = n // 2, (n - 1) // 2
    low = jnp.bfloat16

    def aim(way):
        return {"ctx": right if way == 1 else left}

    barrier = pltpu.get_barrier_semaphore()
    for peer in (left, right):
        pl.semaphore_signal(barrier, inc=1, device_id={"ctx": peer}, device_id_type=MESH)
    pl.semaphore_signal(barrier, inc=1, device_id={"dp": other}, device_id_type=MESH)
    for k in range(1, n_tp):
        pl.semaphore_signal(barrier, inc=1, device_id={"tp": (tp + k) % n_tp}, device_id_type=MESH)
    own_rows = pl.ds(pl.multiple_of(dp * half, half), half)
    loads = [
        pltpu.make_async_copy(source, target, load_sem.at[i])
        for i, (source, target) in enumerate(
            (
                (k_hbm, k_all.at[me]),
                (q_hbm, q_wide),
                (g_hbm, g_wide),
                (o_hbm, o_wide),
                (v_hbm, v_all.at[me]),
                (w_hbm, weight.at[own_rows]),
            )
        )
    ]
    for load in loads:
        load.start()
    pl.semaphore_wait(barrier, 2 + n_tp)
    sends = []
    gathers = {}

    def gather_step(tensor, way, step):
        source, target = ((k_hbm, k_all), (v_hbm, v_all))[tensor]
        row = 2 * tensor + (0 if way == 1 else 1)
        block = member(-way * step)
        if step > 0:
            gathers[row, step - 1].wait_recv()
        count = long if (tensor == 0) == (way == 1) else short
        if step >= count:
            return
        copy = pltpu.make_async_remote_copy(
            src_ref=source if step == 0 else target.at[block],
            dst_ref=target.at[block],
            send_sem=ag_send_sem.at[row, step],
            recv_sem=ag_recv_sem.at[row, step],
            device_id=aim(way),
            device_id_type=MESH,
        )
        copy.start()
        gathers[row, step] = copy
        sends.append(copy)

    gather_step(0, 1, 0)
    gather_step(0, -1, 0)
    w_copy = pltpu.make_async_remote_copy(
        src_ref=w_hbm,
        dst_ref=weight.at[own_rows],
        send_sem=w_sem.at[0],
        recv_sem=w_sem.at[1],
        device_id={"dp": other},
        device_id_type=MESH,
    )
    w_copy.start()

    lane = lax.broadcasted_iota(jnp.int32, (1, toks), 1)
    row_pos = jnp.zeros((1, toks), jnp.int32)
    for piece in range(toks // PIECE):
        here = plan[me * (toks // PIECE) + piece] * PIECE + lane - piece * PIECE
        row_pos = jnp.where(lane // PIECE == piece, here, row_pos)
    start = jnp.zeros((1, toks), jnp.int32)
    end = jnp.int32(0)
    for doc in range(lengths.shape[0]):
        end = end + lengths[doc]
        start = jnp.where(row_pos >= end, end, start)

    def fill(slot, carry):
        key_pos = plan[slot] * PIECE + lax.broadcasted_iota(jnp.int32, (PIECE, toks), 0)
        allowed = (key_pos >= start) & (key_pos <= row_pos)
        bias[pl.ds(pl.multiple_of(slot * PIECE, PIECE), PIECE), :] = jnp.where(allowed, 0.0, NEG)
        return carry

    lax.fori_loop(0, n * toks // PIECE, fill, 0)

    def head_span(h):
        return pl.ds(h * HEAD_SIZE, HEAD_SIZE)

    scale = HEAD_SIZE**-0.5 * math.log2(math.e)

    def score_block(block, first):
        rows = pl.ds(pl.multiple_of(block * toks, toks), toks)
        mask = jnp.concatenate([bias[rows, :]] * per_group, axis=1)
        for g in range(kv_heads):
            raw = lax.dot_general(
                k_all[block, :, head_span(g)], queries[g], NT, preferred_element_type=jnp.float32
            )
            part = raw * scale + mask
            scores[g, rows, :] = part
            high = jnp.max(part.reshape(toks // 8, 8, cols), axis=0)
            top[g] = high if first else jnp.maximum(top[g], high)

    loads[1].wait()
    for g in range(kv_heads):
        for h in range(per_group):
            queries[g, h * toks : (h + 1) * toks, :] = q_wide[:, head_span(g * per_group + h)]
    loads[0].wait()
    score_block(me, True)
    loads[2].wait()
    loads[3].wait()

    def prepare(g):
        for h in range(per_group):
            span = head_span(g * per_group + h)
            grads[g, h * toks : (h + 1) * toks, :] = g_wide[:, span]
            term = g_wide[:, span].astype(jnp.float32) * o_wide[:, span].astype(jnp.float32)
            delta[g, :, h * toks : (h + 1) * toks] = jnp.sum(term.T, axis=0, keepdims=True)

    todo = list(range(kv_heads))
    for step in range(1, long + 1):
        gather_step(0, 1, step)
        if step <= short:
            gather_step(0, -1, step)
        if step >= long - 1 and step - long + 1 < long:
            gather_step(1, 1, step - long + 1)
            gather_step(1, -1, step - long + 1)
        if todo:
            prepare(todo.pop(0))
        score_block(member(-step), False)
        if step <= short:
            score_block(member(step), False)
    for g in todo:
        prepare(g)
    value_steps = list(range(2, long + 1))

    def value_gather():
        if value_steps:
            step = value_steps.pop(0)
            if step <= short:
                gather_step(1, 1, step)
            gather_step(1, -1, step)

    rings = {}

    def ring_step(tensor, g, way, count, step):
        part = v_part if tensor else k_part
        row = 2 * tensor + (0 if way == 1 else 1)
        block = part[g, member(way * (count - step))].astype(jnp.float32)
        if step > 0:
            rings[row, g, step - 1].wait_recv()
            block = block + ring_recv[row, g, step - 1].astype(jnp.float32)
        ring_send[row, g, step] = block.astype(low)
        copy = pltpu.make_async_remote_copy(
            src_ref=ring_send.at[row, g, step],
            dst_ref=ring_recv.at[row, g, step],
            send_sem=ring_send_sem.at[row, g, step],
            recv_sem=ring_recv_sem.at[row, g, step],
            device_id=aim(way),
            device_id_type=MESH,
        )
        copy.start()
        rings[row, g, step] = copy
        sends.append(copy)

    active = []

    def advance():
        for chain in list(active):
            tensor, g, step = chain
            counts = (long, short) if tensor else (short, long)
            for at, way in enumerate((1, -1)):
                if step < counts[at]:
                    ring_step(tensor, g, way, counts[at], step)
            if step == long:
                part = v_part if tensor else k_part
                block = part[g, me].astype(jnp.float32)
                for at in range(2):
                    row = 2 * tensor + at
                    rings[row, g, counts[at] - 1].wait_recv()
                    block = block + ring_recv[row, g, counts[at] - 1].astype(jnp.float32)
                block = block.astype(low)
                if tensor:
                    dv_ref[:, head_span(g)] = block
                    value_grad[:, head_span(g)] = block
                else:
                    dk_ref[:, head_span(g)] = block
                active.remove(chain)
            chain[2] += 1

    segments = 4
    per_segment = n // segments
    for g in range(kv_heads):
        high = jnp.max(top[g], axis=0, keepdims=True)

        def expo(j, total):
            rows = pl.ds(pl.multiple_of(j * toks, toks), toks)
            part = jnp.exp2(scores[g, rows, :] - high)
            scores[g, rows, :] = part
            return total + jnp.sum(part.reshape(toks // 8, 8, cols), axis=0)

        total = lax.fori_loop(0, n, expo, jnp.zeros((8, cols), jnp.float32))
        inverse[g] = 1.0 / jnp.sum(total, axis=0, keepdims=True)
        value_gather()

        def values_of(j, carry):
            rows = pl.ds(pl.multiple_of(j * toks, toks), toks)
            weights = scores[g, rows, :] * inverse[g]
            scores[g, rows, :] = weights
            v_part[g, j] = jnp.dot(
                weights.astype(low), grads[g], preferred_element_type=jnp.float32
            ).astype(low)
            return carry

        lax.fori_loop(0, n, values_of, 0)
        advance()
        active.append([1, g, 0])
    while value_steps:
        value_gather()
    if short == 0 or long == short:
        gather_step(1, 1, short)
    for load in loads[4:]:
        load.wait()
    advance()

    def product(part, c):
        rows = pl.ds(pl.multiple_of(part * share + c * chunk, chunk), chunk)
        return lax.dot_general(
            value_grad[...], weight[rows, :], NT, preferred_element_type=jnp.float32
        ).astype(low)

    parts = {}
    remaining = [(k, c) for c in range(chunks) for k in range(1, n_tp)]

    def send_part():
        if not remaining:
            return
        k, c = remaining.pop(0)
        peer = (tp + k) % n_tp
        part_send[k - 1, c] = product(peer, c)
        copy = pltpu.make_async_remote_copy(
            src_ref=part_send.at[k - 1, c],
            dst_ref=part_recv.at[k - 1, c],
            send_sem=part_send_sem.at[k - 1, c],
            recv_sem=part_recv_sem.at[k - 1, c],
            device_id={"tp": peer},
            device_id_type=MESH,
        )
        copy.start()
        parts[k, c] = copy
        sends.append(copy)

    arrived = False
    for g in range(kv_heads):
        for segment in range(segments):

            def keys_of(j, carry):
                rows = pl.ds(pl.multiple_of(j * toks, toks), toks)
                grad_weights = lax.dot_general(
                    v_all[j, :, head_span(g)], grads[g], NT, preferred_element_type=jnp.float32
                )
                grad_scores = (
                    scores[g, rows, :] * ((grad_weights - delta[g]) * HEAD_SIZE**-0.5)
                ).astype(low)
                k_part[g, j] = jnp.dot(
                    grad_scores, queries[g], preferred_element_type=jnp.float32
                ).astype(low)
                part = lax.dot_general(
                    grad_scores, k_all[j, :, head_span(g)], TN, preferred_element_type=jnp.float32
                )
                dq_acc[...] += part
                return carry

            if segment == 0:
                dq_acc[...] = jnp.zeros_like(dq_acc)
            lax.fori_loop(segment * per_segment, (segment + 1) * per_segment, keys_of, 0)
            if segment == segments - 1:
                active.append([0, g, 0])
            advance()
            if not any(chain[0] for chain in active):
                if not arrived:
                    w_copy.wait()
                    arrived = True
                send_part()
        for h in range(per_group):
            dq_ref[:, head_span(g * per_group + h)] = dq_acc[h * toks : (h + 1) * toks].astype(low)
    while any(chain[0] for chain in active):
        advance()
    if not arrived:
        w_copy.wait()
    while remaining:
        send_part()
        if len(remaining) % 2 == 0:
            advance()
    while active:
        advance()
    for c in range(chunks):
        total = product(tp, c).astype(jnp.float32)
        for k in range(1, n_tp):
            parts[k, c].wait_recv()
            total = total + part_recv[k - 1, c].astype(jnp.float32)
        di_ref[:, c * chunk : (c + 1) * chunk] = total.astype(low)
    for copy in sends:
        copy.wait_send()


def solution(mesh):
    n, n_tp = mesh.shape["ctx"], mesh.shape["tp"]

    def on_device(lengths, plan, queries, keys, values, grads, outputs, weight):
        toks, kv_width = keys.shape[1:]
        q_width = queries.shape[2]
        kv_heads = kv_width // HEAD_SIZE
        cols = q_width // kv_width * toks
        half = weight.shape[0]
        share = 2 * half // n_tp
        chunk = 512
        chunks = share // chunk
        steps = n // 2
        low, wide = jnp.bfloat16, jnp.float32
        vmem = pl.BlockSpec(memory_space=pltpu.VMEM)
        smem = pl.BlockSpec(memory_space=pltpu.SMEM)
        hbm = pl.BlockSpec(memory_space=pl.ANY)
        narrow = jax.ShapeDtypeStruct((toks, kv_width), low)
        dma = pltpu.SemaphoreType.DMA
        query_grad, key_grad, value_grad, input_grad = pl.pallas_call(
            functools.partial(fused_kernel, n, n_tp, chunk),
            out_shape=(
                jax.ShapeDtypeStruct((toks, q_width), low),
                narrow,
                narrow,
                jax.ShapeDtypeStruct((toks, share), low),
            ),
            in_specs=[smem] * 2 + [hbm] * 6,
            out_specs=[vmem] * 4,
            scratch_shapes=[
                pltpu.VMEM((toks, q_width), low),
                pltpu.VMEM((toks, q_width), low),
                pltpu.VMEM((toks, q_width), low),
                pltpu.VMEM((n, toks, kv_width), low),
                pltpu.VMEM((n, toks, kv_width), low),
                pltpu.VMEM((kv_heads, cols, HEAD_SIZE), low),
                pltpu.VMEM((kv_heads, cols, HEAD_SIZE), low),
                pltpu.VMEM((kv_heads, 1, cols), wide),
                pltpu.VMEM((n * toks, toks), wide),
                pltpu.VMEM((kv_heads, n * toks, cols), wide),
                pltpu.VMEM((kv_heads, 8, cols), wide),
                pltpu.VMEM((kv_heads, 1, cols), wide),
                pltpu.VMEM((cols, HEAD_SIZE), wide),
                pltpu.VMEM((kv_heads, n, toks, HEAD_SIZE), low),
                pltpu.VMEM((kv_heads, n, toks, HEAD_SIZE), low),
                pltpu.VMEM((toks, kv_width), low),
                pltpu.VMEM((2 * half, kv_width), low),
                pltpu.VMEM((4, kv_heads, steps, toks, HEAD_SIZE), low),
                pltpu.VMEM((4, kv_heads, steps, toks, HEAD_SIZE), low),
                pltpu.VMEM((n_tp - 1, chunks, toks, chunk), low),
                pltpu.VMEM((n_tp - 1, chunks, toks, chunk), low),
                dma((6,)),
                dma((4, steps)),
                dma((4, steps)),
                dma((4, kv_heads, steps)),
                dma((4, kv_heads, steps)),
                dma((n_tp - 1, chunks)),
                dma((n_tp - 1, chunks)),
                dma((2,)),
            ],
            compiler_params=pltpu.CompilerParams(
                collective_id=0, has_side_effects=True, vmem_limit_bytes=VMEM_LIMIT
            ),
            name="fused_backward",
        )(lengths[0], plan[0], queries[0], grads[0], outputs[0], keys[0], values[0], weight)
        return query_grad[None], key_grad[None], value_grad[None], input_grad[None]

    spread = P("dp", "ctx", "tp")
    return jax.shard_map(
        on_device,
        mesh=mesh,
        in_specs=(P("dp", None), P("dp", None)) + (spread,) * 5 + (P("dp", "tp"),),
        out_specs=(spread,) * 4,
        check_vma=False,
    )
```

time: 324 us -> 122 us (0.38)
  waiting for transfers between devices: 206 us -> 0 us
  Pallas kernels: 0 us -> 114 us
  matrix products: 63.3 us -> 0 us
  local copies, waits for them, and re-layouts: 25.4 us -> 7.71 us
  between operations: 15.3 us -> 0.64 us
  other arithmetic: 13.8 us -> 0 us
    reduce_scatter x3 -> x0, waiting for transfers between devices: 150 us -> none  [the longest x1 59.3 us: on_device(): lax.psum_scatter(value_part.astype(jnp.bfloat16), 'ctx', scatter_dimensio...]
    pallas_call x0 -> x1, Pallas kernels: none -> 114 us  [on_device(): pl.pallas_call(functools.partial(fused_kernel, n, n_tp, chunk), out_shape...]
    dot_general x13 -> x0, matrix products: 63.3 us -> none  [the longest x4 18.4 us: block_scores(): jnp.einsum('tkgd,skd->kgts', head_queries, head_keys, preferred_element_t...]
    all_gather x3 -> x0, waiting for transfers between devices: 53.5 us -> none  [the longest x1 33.3 us: on_device(): lax.all_gather(rotated_keys[0], 'ctx', axis=0, tiled=True)]
    reduce_sum x4 -> x0, other arithmetic: 11.2 us -> none  [the longest x2 9.24 us: stats_step(): jnp.sum(jnp.where(allowed, jnp.exp(masked - new_max[..., None]), 0.0), ax...]
    while x30 -> x0, local copies, waits for them, and re-layouts: 7.83 us -> none
    convert_element_type x3 -> x0, local copies, waits for them, and re-layouts: 7.69 us -> none  [the longest x1 2.99 us: on_device(): head_output.astype(jnp.float32)]
    unnamed x8 -> x4, local copies, waits for them, and re-layouts: 5.39 us -> 7.71 us
  transfers between devices with their start and end apart: 6 -> 0, of which waited for: 5 -> 0; matrix products, arithmetic and copies ran while one was open for 13% -> 0% of each run, Pallas kernels for 0% -> 0%
where the time goes in v2:
time: 122 us
  Pallas kernels  114 us (93%)
  local copies, waits for them, and re-layouts  7.71 us (6%)
    pallas_call x1, Pallas kernels, on_device(): pl.pallas_call(functools.partial(fused_kernel, n, n_tp, chunk), out_shape...  114 us
    unnamed x4, local copies, waits for them, and re-layouts  7.71 us

profile of v2, /device:TPU:0, one launch (start us, length us, event | category | flops | bytes accessed | tf_op | source)
XLA Modules:
  0.0 122.1 jit_solution(3647589984295086457)
XLA Ops:
  0.6 113.8 %fused_backward.1 = (bf16[128,4096]{1,0:T(8,128)(2,1)}, bf16[128,512]{1,0:T(8,128)(2,1)}, bf16[128,512]{1,0:T(8,128)(2,1)}, bf16[128,4096]{1,0:T(8,128)(2,1)}) custom-call(s32[4]{0:T(128)} %bitcast.20, s32[16]{0:T(128)} %bitcast.21, bf16[128,4096]{1,0:T(8,128)(2,1)} %bitcast.13, bf16[128,4096]{1,0:T(8,128)(2,1)} %bitcast.14, bf16[128,4096]{1,0:T(8,128)(2,1)} %bitcast.15, ...), custom_call_target="tpu_custom_call" | custom-call | tf_op jit(solution)/shard_map/fused_backward/pallas_call | solution.py:422
  114.4 2.3 %copy.16 = bf16[1,128,4096]{2,1,0:T(8,128)(2,1)} copy(bf16[1,128,4096]{2,1,0:T(8,128)(2,1)} %bitcast.12) | data formatting | bytes 2097152
  116.7 1.6 %copy.17 = bf16[1,128,512]{2,1,0:T(8,128)(2,1)} copy(bf16[1,128,512]{2,1,0:T(8,128)(2,1)} %bitcast.19) | data formatting | bytes 262144
  118.3 1.6 %copy.18 = bf16[1,128,512]{2,1,0:T(8,128)(2,1)} copy(bf16[1,128,512]{2,1,0:T(8,128)(2,1)} %bitcast.18) | data formatting | bytes 262144
  119.9 2.3 %copy.19 = bf16[1,128,4096]{2,1,0:T(8,128)(2,1)} copy(bf16[1,128,4096]{2,1,0:T(8,128)(2,1)} %bitcast.11) | data formatting | bytes 2097152

commit v3 on v2

--- a/solution.py
+++ b/solution.py
@@ -72,15 +72,14 @@
     v_part,
     value_grad,
     weight,
-    ring_send,
-    ring_recv,
+    term_recv,
     part_send,
     part_recv,
     load_sem,
     ag_send_sem,
     ag_recv_sem,
-    ring_send_sem,
-    ring_recv_sem,
+    term_send_sem,
+    term_recv_sem,
     part_send_sem,
     part_recv_sem,
     w_sem,
@@ -103,8 +102,8 @@
         return {"ctx": right if way == 1 else left}
 
     barrier = pltpu.get_barrier_semaphore()
-    for peer in (left, right):
-        pl.semaphore_signal(barrier, inc=1, device_id={"ctx": peer}, device_id_type=MESH)
+    for k in range(1, n):
+        pl.semaphore_signal(barrier, inc=1, device_id={"ctx": (me + k) % n}, device_id_type=MESH)
     pl.semaphore_signal(barrier, inc=1, device_id={"dp": other}, device_id_type=MESH)
     for k in range(1, n_tp):
         pl.semaphore_signal(barrier, inc=1, device_id={"tp": (tp + k) % n_tp}, device_id_type=MESH)
@@ -124,7 +123,7 @@
     ]
     for load in loads:
         load.start()
-    pl.semaphore_wait(barrier, 2 + n_tp)
+    pl.semaphore_wait(barrier, n - 1 + n_tp)
     sends = []
     gathers = {}
 
@@ -149,8 +148,9 @@
         gathers[row, step] = copy
         sends.append(copy)
 
-    gather_step(0, 1, 0)
-    gather_step(0, -1, 0)
+    for tensor in range(2):
+        gather_step(tensor, 1, 0)
+        gather_step(tensor, -1, 0)
     w_copy = pltpu.make_async_remote_copy(
         src_ref=w_hbm,
         dst_ref=weight.at[own_rows],
@@ -218,9 +218,8 @@
         gather_step(0, 1, step)
         if step <= short:
             gather_step(0, -1, step)
-        if step >= long - 1 and step - long + 1 < long:
-            gather_step(1, 1, step - long + 1)
-            gather_step(1, -1, step - long + 1)
+            gather_step(1, 1, step)
+        gather_step(1, -1, step)
         if todo:
             prepare(todo.pop(0))
         score_block(member(-step), False)
@@ -228,64 +227,36 @@
             score_block(member(step), False)
     for g in todo:
         prepare(g)
-    value_steps = list(range(2, long + 1))
-
-    def value_gather():
-        if value_steps:
-            step = value_steps.pop(0)
-            if step <= short:
-                gather_step(1, 1, step)
-            gather_step(1, -1, step)
-
-    rings = {}
-
-    def ring_step(tensor, g, way, count, step):
+    terms = {}
+
+    def scatter(tensor, g):
         part = v_part if tensor else k_part
-        row = 2 * tensor + (0 if way == 1 else 1)
-        block = part[g, member(way * (count - step))].astype(jnp.float32)
-        if step > 0:
-            rings[row, g, step - 1].wait_recv()
-            block = block + ring_recv[row, g, step - 1].astype(jnp.float32)
-        ring_send[row, g, step] = block.astype(low)
-        copy = pltpu.make_async_remote_copy(
-            src_ref=ring_send.at[row, g, step],
-            dst_ref=ring_recv.at[row, g, step],
-            send_sem=ring_send_sem.at[row, g, step],
-            recv_sem=ring_recv_sem.at[row, g, step],
-            device_id=aim(way),
-            device_id_type=MESH,
-        )
-        copy.start()
-        rings[row, g, step] = copy
-        sends.append(copy)
-
-    active = []
-
-    def advance():
-        for chain in list(active):
-            tensor, g, step = chain
-            counts = (long, short) if tensor else (short, long)
-            for at, way in enumerate((1, -1)):
-                if step < counts[at]:
-                    ring_step(tensor, g, way, counts[at], step)
-            if step == long:
-                part = v_part if tensor else k_part
-                block = part[g, me].astype(jnp.float32)
-                for at in range(2):
-                    row = 2 * tensor + at
-                    rings[row, g, counts[at] - 1].wait_recv()
-                    block = block + ring_recv[row, g, counts[at] - 1].astype(jnp.float32)
-                block = block.astype(low)
-                if tensor:
-                    dv_ref[:, head_span(g)] = block
-                    value_grad[:, head_span(g)] = block
-                else:
-                    dk_ref[:, head_span(g)] = block
-                active.remove(chain)
-            chain[2] += 1
-
-    segments = 4
-    per_segment = n // segments
+        for k in range(1, n):
+            peer = (me + k) % n
+            copy = pltpu.make_async_remote_copy(
+                src_ref=part.at[g, peer],
+                dst_ref=term_recv.at[tensor, g, k - 1],
+                send_sem=term_send_sem.at[tensor, g, k - 1],
+                recv_sem=term_recv_sem.at[tensor, g, k - 1],
+                device_id={"ctx": peer},
+                device_id_type=MESH,
+            )
+            copy.start()
+            terms[tensor, g, k] = copy
+            sends.append(copy)
+
+    def collect(tensor, g):
+        block = (v_part if tensor else k_part)[g, me].astype(jnp.float32)
+        for k in range(1, n):
+            terms[tensor, g, k].wait_recv()
+            block = block + term_recv[tensor, g, k - 1].astype(jnp.float32)
+        block = block.astype(low)
+        if tensor:
+            dv_ref[:, head_span(g)] = block
+            value_grad[:, head_span(g)] = block
+        else:
+            dk_ref[:, head_span(g)] = block
+
     for g in range(kv_heads):
         high = jnp.max(top[g], axis=0, keepdims=True)
 
@@ -297,8 +268,6 @@
 
         total = lax.fori_loop(0, n, expo, jnp.zeros((8, cols), jnp.float32))
         inverse[g] = 1.0 / jnp.sum(total, axis=0, keepdims=True)
-        value_gather()
-
         def values_of(j, carry):
             rows = pl.ds(pl.multiple_of(j * toks, toks), toks)
             weights = scores[g, rows, :] * inverse[g]
@@ -309,15 +278,9 @@
             return carry
 
         lax.fori_loop(0, n, values_of, 0)
-        advance()
-        active.append([1, g, 0])
-    while value_steps:
-        value_gather()
-    if short == 0 or long == short:
-        gather_step(1, 1, short)
+        scatter(1, g)
     for load in loads[4:]:
         load.wait()
-    advance()
 
     def product(part, c):
         rows = pl.ds(pl.multiple_of(part * share + c * chunk, chunk), chunk)
@@ -326,12 +289,8 @@
         ).astype(low)
 
     parts = {}
-    remaining = [(k, c) for c in range(chunks) for k in range(1, n_tp)]
-
-    def send_part():
-        if not remaining:
-            return
-        k, c = remaining.pop(0)
+
+    def send_part(k, c):
         peer = (tp + k) % n_tp
         part_send[k - 1, c] = product(peer, c)
         copy = pltpu.make_async_remote_copy(
@@ -346,56 +305,45 @@
         parts[k, c] = copy
         sends.append(copy)
 
-    arrived = False
     for g in range(kv_heads):
-        for segment in range(segments):
-
-            def keys_of(j, carry):
-                rows = pl.ds(pl.multiple_of(j * toks, toks), toks)
-                grad_weights = lax.dot_general(
-                    v_all[j, :, head_span(g)], grads[g], NT, preferred_element_type=jnp.float32
-                )
-                grad_scores = (
-                    scores[g, rows, :] * ((grad_weights - delta[g]) * HEAD_SIZE**-0.5)
-                ).astype(low)
-                k_part[g, j] = jnp.dot(
-                    grad_scores, queries[g], preferred_element_type=jnp.float32
-                ).astype(low)
-                part = lax.dot_general(
-                    grad_scores, k_all[j, :, head_span(g)], TN, preferred_element_type=jnp.float32
-                )
-                dq_acc[...] += part
-                return carry
-
-            if segment == 0:
-                dq_acc[...] = jnp.zeros_like(dq_acc)
-            lax.fori_loop(segment * per_segment, (segment + 1) * per_segment, keys_of, 0)
-            if segment == segments - 1:
-                active.append([0, g, 0])
-            advance()
-            if not any(chain[0] for chain in active):
-                if not arrived:
-                    w_copy.wait()
-                    arrived = True
-                send_part()
+        if g == kv_heads - 1:
+            for group in range(kv_heads):
+                collect(1, group)
+            w_copy.wait()
+            for c in range(chunks):
+                for k in range(1, n_tp):
+                    send_part(k, c)
+
+        def keys_of(j, carry):
+            rows = pl.ds(pl.multiple_of(j * toks, toks), toks)
+            grad_weights = lax.dot_general(
+                v_all[j, :, head_span(g)], grads[g], NT, preferred_element_type=jnp.float32
+            )
+            grad_scores = (
+                scores[g, rows, :] * ((grad_weights - delta[g]) * HEAD_SIZE**-0.5)
+            ).astype(low)
+            k_part[g, j] = jnp.dot(
+                grad_scores, queries[g], preferred_element_type=jnp.float32
+            ).astype(low)
+            part = lax.dot_general(
+                grad_scores, k_all[j, :, head_span(g)], TN, preferred_element_type=jnp.float32
+            )
+            dq_acc[...] += part
+            return carry
+
+        dq_acc[...] = jnp.zeros_like(dq_acc)
+        lax.fori_loop(0, n, keys_of, 0)
+        scatter(0, g)
         for h in range(per_group):
             dq_ref[:, head_span(g * per_group + h)] = dq_acc[h * toks : (h + 1) * toks].astype(low)
-    while any(chain[0] for chain in active):
-        advance()
-    if not arrived:
-        w_copy.wait()
-    while remaining:
-        send_part()
-        if len(remaining) % 2 == 0:
-            advance()
-    while active:
-        advance()
     for c in range(chunks):
         total = product(tp, c).astype(jnp.float32)
         for k in range(1, n_tp):
             parts[k, c].wait_recv()
             total = total + part_recv[k - 1, c].astype(jnp.float32)
         di_ref[:, c * chunk : (c + 1) * chunk] = total.astype(low)
+    for g in range(kv_heads):
+        collect(0, g)
     for copy in sends:
         copy.wait_send()
 
@@ -447,15 +395,14 @@
                 pltpu.VMEM((kv_heads, n, toks, HEAD_SIZE), low),
                 pltpu.VMEM((toks, kv_width), low),
                 pltpu.VMEM((2 * half, kv_width), low),
-                pltpu.VMEM((4, kv_heads, steps, toks, HEAD_SIZE), low),
-                pltpu.VMEM((4, kv_heads, steps, toks, HEAD_SIZE), low),
+                pltpu.VMEM((2, kv_heads, n - 1, toks, HEAD_SIZE), low),
                 pltpu.VMEM((n_tp - 1, chunks, toks, chunk), low),
                 pltpu.VMEM((n_tp - 1, chunks, toks, chunk), low),
                 dma((6,)),
                 dma((4, steps)),
                 dma((4, steps)),
-                dma((4, kv_heads, steps)),
-                dma((4, kv_heads, steps)),
+                dma((2, kv_heads, n - 1)),
+                dma((2, kv_heads, n - 1)),
                 dma((n_tp - 1, chunks)),
                 dma((n_tp - 1, chunks)),
                 dma((2,)),

time: 122 us -> 95.8 us (0.79)
  the two profiles are of different devices: /device:TPU:0 before, /device:TPU:12 now
where the time goes in v3:
time: 95.8 us; the launch traced here: 95.5 us
  Pallas kernels  87.2 us (91%)
  local copies, waits for them, and re-layouts  7.71 us (8%)
    pallas_call x1, Pallas kernels, on_device(): pl.pallas_call(functools.partial(fused_kernel, n, n_tp, chunk), out_shape...  87.2 us
    unnamed x4, local copies, waits for them, and re-layouts  7.71 us

profile of v3, /device:TPU:12, one launch (start us, length us, event | category | flops | bytes accessed | tf_op | source)
XLA Modules:
  0.0 95.5 jit_solution(657036248529660474)
XLA Ops:
  0.6 87.2 %fused_backward.1 = (bf16[128,4096]{1,0:T(8,128)(2,1)}, bf16[128,512]{1,0:T(8,128)(2,1)}, bf16[128,512]{1,0:T(8,128)(2,1)}, bf16[128,4096]{1,0:T(8,128)(2,1)}) custom-call(s32[4]{0:T(128)} %bitcast.20, s32[16]{0:T(128)} %bitcast.21, bf16[128,4096]{1,0:T(8,128)(2,1)} %bitcast.13, bf16[128,4096]{1,0:T(8,128)(2,1)} %bitcast.14, bf16[128,4096]{1,0:T(8,128)(2,1)} %bitcast.15, ...), custom_call_target="tpu_custom_call" | custom-call | tf_op jit(solution)/shard_map/fused_backward/pallas_call | solution.py:370
  87.8 2.3 %copy.16 = bf16[1,128,4096]{2,1,0:T(8,128)(2,1)} copy(bf16[1,128,4096]{2,1,0:T(8,128)(2,1)} %bitcast.12) | data formatting | bytes 2097152
  90.1 1.6 %copy.17 = bf16[1,128,512]{2,1,0:T(8,128)(2,1)} copy(bf16[1,128,512]{2,1,0:T(8,128)(2,1)} %bitcast.19) | data formatting | bytes 262144
  91.7 1.6 %copy.18 = bf16[1,128,512]{2,1,0:T(8,128)(2,1)} copy(bf16[1,128,512]{2,1,0:T(8,128)(2,1)} %bitcast.18) | data formatting | bytes 262144
  93.2 2.3 %copy.19 = bf16[1,128,4096]{2,1,0:T(8,128)(2,1)} copy(bf16[1,128,4096]{2,1,0:T(8,128)(2,1)} %bitcast.11) | data formatting | bytes 2097152

commit v4 on v3

--- a/solution.py
+++ b/solution.py
@@ -346,6 +346,29 @@
         collect(0, g)
     for copy in sends:
         copy.wait_send()
+
+
+def place_kernel(*refs):
+    count = len(refs) // 2
+    copies = [
+        pltpu.make_async_copy(refs[i], refs[count + i], refs[-1].at[i]) for i in range(count)
+    ]
+    for copy in copies:
+        copy.start()
+    for copy in copies:
+        copy.wait()
+
+
+def place(arrays):
+    hbm = pl.BlockSpec(memory_space=pl.ANY)
+    return pl.pallas_call(
+        place_kernel,
+        out_shape=tuple(jax.ShapeDtypeStruct(a.shape, a.dtype) for a in arrays),
+        in_specs=[hbm] * len(arrays),
+        out_specs=[hbm] * len(arrays),
+        scratch_shapes=[pltpu.SemaphoreType.DMA((len(arrays),))],
+        name="place_results",
+    )(*arrays)
 
 
 def solution(mesh):
@@ -412,6 +435,9 @@
             ),
             name="fused_backward",
         )(lengths[0], plan[0], queries[0], grads[0], outputs[0], keys[0], values[0], weight)
+        query_grad, key_grad, value_grad, input_grad = place(
+            (query_grad, key_grad, value_grad, input_grad)
+        )
         return query_grad[None], key_grad[None], value_grad[None], input_grad[None]
 
     spread = P("dp", "ctx", "tp")

time: 95.8 us -> 161 us (1.68)
  the two profiles are of different devices: /device:TPU:12 before, /device:TPU:0 now
where the time goes in v4:
time: 161 us; the launch traced here: 158 us
  Pallas kernels  157 us (98%)
    pallas_call x1, Pallas kernels, on_device(): pl.pallas_call(functools.partial(fused_kernel, n, n_tp, chunk), out_shape...  84.8 us
    pallas_call x1, Pallas kernels, place(): pl.pallas_call(place_kernel, out_shape=tuple((jax.ShapeDtypeStruct(a.shap...  72.6 us

profile of v4, /device:TPU:0, one launch (start us, length us, event | category | flops | bytes accessed | tf_op | source)
XLA Modules:
  0.0 158.1 jit_solution(11021205693606931884)
XLA Ops:
  0.6 84.8 %fused_backward.1 = (bf16[128,4096]{1,0:T(8,128)(2,1)}, bf16[128,512]{1,0:T(8,128)(2,1)}, bf16[128,512]{1,0:T(8,128)(2,1)}, bf16[128,4096]{1,0:T(8,128)(2,1)}) custom-call(s32[4]{0:T(128)} %bitcast.16, s32[16]{0:T(128)} %bitcast.17, bf16[128,4096]{1,0:T(8,128)(2,1)} %bitcast.11, bf16[128,4096]{1,0:T(8,128)(2,1)} %bitcast.12, bf16[128,4096]{1,0:T(8,128)(2,1)} %bitcast.13, ...), custom_call_target="tpu_custom_call" | custom-call | tf_op jit(solution)/shard_map/fused_backward/pallas_call | solution.py:393
  85.4 72.6 %place_results.1 = (bf16[128,4096]{1,0:T(8,128)(2,1)}, bf16[128,512]{1,0:T(8,128)(2,1)}, bf16[128,512]{1,0:T(8,128)(2,1)}, bf16[128,4096]{1,0:T(8,128)(2,1)}) custom-call(bf16[128,4096]{1,0:T(8,128)(2,1)} %get-tuple-element.12.refs_0_, bf16[128,512]{1,0:T(8,128)(2,1)} %get-tuple-element.13.refs_1_, bf16[128,512]{1,0:T(8,128)(2,1)} %get-tuple-element.14.refs_2_, ...), custom_call_target="tpu_custom_call" | custom-call | tf_op jit(solution)/shard_map/place_results/pallas_call | solution.py:364
